TPU v7x, 32 devices: a whole 2x2x4 slice. The times are simulated.
32 devices in a mesh: dp: 2 (over core), tensor: 16 (over z, y, x).
Axes of the slice: x: 2, y: 2, z: 4, core: 2. Of those that a mesh axis runs over, the one named last changes fastest.
Arguments:
- gate_pre: bfloat16 [1024, 16384], P('dp', 'tensor'), may hold values from -6 to 6
- up_pre: bfloat16 [1024, 16384], P('dp', 'tensor'), may hold values from -6 to 6
- down_weight: bfloat16 [16384, 4096], P('tensor'), may hold values from -0.0625 to 0.0625
- block_mask: int32 [128, 32], P('tensor'), may hold values from 0 to 1, as said below
- out_grad: bfloat16 [1024, 4096], P(('dp', 'tensor')), may hold values from -6 to 6
Outputs:
- layer_out: bfloat16 [1024, 4096], P(('dp', 'tensor'))
- gate_grad: bfloat16 [1024, 16384], P('dp', 'tensor')
- up_grad: bfloat16 [1024, 16384], P('dp', 'tensor')
- weight_grad: bfloat16 [16384, 4096], P('tensor')
Inputs may be any that keep to these rules, and one draw needn't show every extreme that they name: `block_mask`: each tensor shard's 8 x 32 blocks hold between 64 and 192 kept blocks; in every draw some shard keeps exactly 192.
All inputs are finite; a program needn't handle non-finite values.
Results may differ from a plain program's by a relative error of at most 0.0049.
Values may be sent and summed in bfloat16 or wider, within the bound.
A program may use at most 128 MiB of HBM per device.

v0:
```python
import math

import jax
import jax.numpy as jnp
from jax import lax
from jax.sharding import PartitionSpec as P


def local(gate_pre, up_pre, down_weight, block_mask, out_grad):
    blk_rows, blk_cols = block_mask.shape
    ff_local, width = down_weight.shape
    masked = (
        down_weight.reshape(blk_rows, 128, blk_cols, 128)
        * block_mask.astype(jnp.bfloat16)[:, None, :, None]
    ).reshape(ff_local, width)
    gate_val = gate_pre.astype(jnp.float32)
    up_val = up_pre.astype(jnp.float32)
    sigmoid_gate = jax.nn.sigmoid(gate_val)
    silu_gate = gate_val * sigmoid_gate
    hidden = (silu_gate * up_val).astype(jnp.bfloat16)
    layer_out = lax.psum_scatter(
        jnp.dot(hidden, masked, preferred_element_type=jnp.float32),
        "tensor",
        scatter_dimension=0,
        tiled=True,
    ).astype(jnp.bfloat16)
    cot_rows = lax.all_gather(out_grad, "tensor", axis=0, tiled=True)
    hidden_grad = lax.dot_general(
        cot_rows, masked, (((1,), (1,)), ((), ())), preferred_element_type=jnp.float32
    )
    gate_grad = (
        hidden_grad * up_val * sigmoid_gate * (1.0 + gate_val * (1.0 - sigmoid_gate))
    ).astype(jnp.bfloat16)
    up_grad = (hidden_grad * silu_gate).astype(jnp.bfloat16)
    tokens_all = out_grad.shape[0] * lax.axis_size("tensor") * lax.axis_size("dp")
    grad_scale = 1.0 / math.sqrt(tokens_all)
    partial_grad = (
        lax.dot_general(
            hidden, cot_rows, (((0,), (0,)), ((), ())), preferred_element_type=jnp.float32
        )
        * grad_scale
    )
    blocked = (
        partial_grad.reshape(blk_rows, 128, blk_cols, 128)
        * block_mask.astype(jnp.float32)[:, None, :, None]
    )
    summed = lax.psum(blocked.reshape(ff_local, width), "dp")
    weight_grad = summed.astype(jnp.bfloat16)
    return (layer_out, gate_grad, up_grad, weight_grad)


def solution(mesh):
    return jax.shard_map(
        local,
        mesh=mesh,
        in_specs=(
            P("dp", "tensor"),
            P("dp", "tensor"),
            P("tensor", None),
            P("tensor", None),
            P(("dp", "tensor"), None),
        ),
        out_specs=(
            P(("dp", "tensor"), None),
            P("dp", "tensor"),
            P("dp", "tensor"),
            P("tensor", None),
        ),
        check_vma=False,
    )
```

profile of v0, /device:TPU:0, one launch (start us, length us, event | category | flops | bytes accessed | tf_op | source)
XLA Modules:
  0.0 277.0 jit_solution(12669702746729950555)
XLA Ops:
  7.2 0.0 copy-start.2
  7.2 0.0 all-gather.2.cloned.1.call-start
  7.2 0.7 all-gather.2.cloned.1.call-update
  7.9 0.0 reduce-scatter.2.cloned.1.call-start
  8.0 1.5 copy.9
  9.5 1.5 copy.10
  11.0 0.0 copy-done.2
  11.0 0.0 copy-start.3
  11.0 1.1 mul.51
  12.2 0.0 copy-start
  12.2 4.2 %copy-done = bf16[8,128,32,128]{3,2,1,0:T(8,128)(2,1)} copy-done((bf16[8,128,32,128]{3,2,1,0:T(8,128)(2,1)}, bf16[8,128,32,128]{3,2,1,0:T(8,128)(2,1)S(1)}, u32[]{:S(2)}) %copy-start) | copy-done | bytes 8388632
  16.4 1.0 copy-done.3
  17.4 15.1 %fusion.1 = f32[512,4096]{1,0:T(8,128)} fusion(bf16[1024,4096]{1,0:T(8,128)(2,1)S(1)} %copy-done.3, bf16[128,8,32,128]{3,2,1,0:T(8,128)(2,1)S(1)} %bitcast.20, bf16[512,1024]{0,1:T(8,128)(2,1)S(1)} %copy.10, bf16[512,1024]{0,1:T(8,128)(2,1)S(1)} %copy.9), kind=kOutput, calls=%fused_computation.8 | convolution fusion | flops 4303355904 | bytes 27262976 | tf_op jit(solution)/shard_map/dot_general | solution.py:22
  32.4 0.0 reduce-scatter.2.cloned.1.call-update
  32.5 57.1 %all-gather.2.cloned.1.call-done = bf16[512,4096]{1,0:T(8,128)(2,1)} async-done(((bf16[32,4096]{1,0:T(8,128)(2,1)}), bf16[512,4096]{1,0:T(8,128)(2,1)}) %all-gather.2.cloned.1.call-update) | async-done | bytes 4194320 | tf_op jit(solution)/shard_map/all_gather | solution.py:27
  89.6 14.0 %fusion.10 = (bf16[512,1024]{0,1:T(8,128)(2,1)}, bf16[512,1024]{0,1:T(8,128)(2,1)S(1)}) fusion(bf16[512,1024]{0,1:T(8,128)(2,1)S(1)} %copy.9, bf16[512,1024]{0,1:T(8,128)(2,1)S(1)} %copy.10, bf16[512,4096]{1,0:T(8,128)(2,1)} %all-gather.2.cloned.1.call-done, bf16[1024,4096]{1,0:T(8,128)(2,1)} %param.7, bf16[128,8,32,128]{3,2,1,0:T(8,128)(2,1)} %bitcast.21), kind=kOutput, calls=%fused_computation.18 | convolution fusion | flops 4307025920 | bytes 25165824 | tf_op jit(solution)/shard_map/dot_general | solution.py:28
  103.6 2.3 copy.12
  105.8 1.3 copy.11
  107.1 0.0 copy-start.1
  107.1 7.9 %mul.61 = f32[8,128,32,128]{3,2,1,0:T(8,128)} broadcast(f32[8,32]{1,0:T(8,128)S(1)} %get-tuple-element.10), dimensions={0,2} | broadcast | bytes 16778240 | tf_op jit(solution)/shard_map/mul | solution.py:44
  115.1 0.0 copy-done.1
  115.1 17.3 %bitcast_multiply_fusion = f32[1024,4096]{1,0:T(8,128)} fusion(f32[128,8,32,128]{3,2,1,0:T(8,128)} %bitcast.19, bf16[512,4096]{1,0:T(8,128)(2,1)S(1)} %copy-done.1, bf16[512,1024]{0,1:T(8,128)(2,1)S(1)} %copy.10, bf16[512,1024]{0,1:T(8,128)(2,1)S(1)} %copy.9), kind=kOutput, calls=%fused_computation | convolution fusion | flops 4307550208 | bytes 39845888 | tf_op jit(solution)/shard_map/dot_general | solution.py:38
  132.4 46.2 %all-reduce.1 = bf16[1024,4096]{1,0:T(8,128)(2,1)} all-reduce(f32[1024,4096]{1,0:T(8,128)} %bitcast_multiply_fusion), channel_id=1, replica_groups=mesh['dp'=2,'tensor'=16] {'dp'}, use_global_device_ids=true, to_apply=%region_1.0 | all-reduce | flops 4194304 | bytes 25165824 | tf_op jit(solution)/shard_map/psum | solution.py:47
  178.6 89.8 %reduce-scatter.2.cloned.1.call-done = f32[32,4096]{1,0:T(8,128)} async-done(((f32[512,4096]{1,0:T(8,128)}), f32[32,4096]{1,0:T(8,128)}) %reduce-scatter.2.cloned.1.call-update) | async-done | bytes 524304 | tf_op jit(solution)/shard_map/reduce_scatter | solution.py:21
  268.3 1.8 convert_element_type.31
  (1 shorter events, 0.0 us)
Async XLA Ops:
  7.2 3.8 %copy-start.2 = (s32[8,32]{1,0:T(8,128)S(1)}, s32[8,32]{1,0:T(8,128)}, u32[]{:S(2)}) copy-start(s32[8,32]{1,0:T(8,128)} %param.8) | copy-start | bytes 3076
  7.2 82.4 %all-gather.2.cloned.1.call-start = ((), (), s32[]{:S(2)}) async-start(), calls=%async_computation.2 | async-start | bytes 4456448 | tf_op jit(solution)/shard_map/all_gather | solution.py:27
  7.9 260.4 %reduce-scatter.2.cloned.1.call-start = ((), (), s32[]{:S(2)}) async-start(), calls=%async_computation.1 | async-start | bytes 8912896 | tf_op jit(solution)/shard_map/reduce_scatter | solution.py:21
  11.0 6.4 %copy-start.3 = (bf16[1024,4096]{1,0:T(8,128)(2,1)S(1)}, bf16[1024,4096]{1,0:T(8,128)(2,1)}, u32[]{:S(2)}) copy-start(bf16[1024,4096]{1,0:T(8,128)(2,1)} %param.7) | copy-start | bytes 25165828
  12.2 4.3 %copy-start = (bf16[8,128,32,128]{3,2,1,0:T(8,128)(2,1)}, bf16[8,128,32,128]{3,2,1,0:T(8,128)(2,1)S(1)}, u32[]{:S(2)}) copy-start(bf16[8,128,32,128]{3,2,1,0:T(8,128)(2,1)S(1)} %mul.51) | copy-start | bytes 25165828
  107.1 7.9 %copy-start.1 = (bf16[512,4096]{1,0:T(8,128)(2,1)S(1)}, bf16[512,4096]{1,0:T(8,128)(2,1)}, u32[]{:S(2)}) copy-start(bf16[512,4096]{1,0:T(8,128)(2,1)} %all-gather.2.cloned.1.call-done) | copy-start | bytes 12582916
Sparse Core Ops, SparseCore 0:
  10.8 78.7 all-gather.1
  91.9 176.4 reduce-scatter.1
where the time goes:
time: 279 us; the launch traced here: 277 us
  waiting for transfers between devices  148 us (53%)
  matrix products  46.3 us (17%)
  blocking collectives  46.2 us (17%)
  local copies, waits for them, and re-layouts  20.9 us (7%)
  between operations  14.1 us (5%)
    reduce_scatter x1, waiting for transfers between devices, local(): lax.psum_scatter(jnp.dot(hidden, masked, preferred_element_type=jnp.float...  89.8 us
    all_gather x1, waiting for transfers between devices, local(): cot_rows = lax.all_gather(out_grad, 'tensor', axis=0, tiled=True)  57.1 us
    psum x1, blocking collectives, local(): summed = lax.psum(blocked.reshape(ff_local, width), 'dp')  46.2 us
    dot_general x1, matrix products, local(): lax.dot_general(hidden, cot_rows, (((0,), (0,)), ((), ())), preferred_ele...  17.3 us
    dot_general x1, matrix products, local(): jnp.dot(hidden, masked, preferred_element_type=jnp.float32)  15.1 us
    dot_general x1, matrix products, local(): lax.dot_general(cot_rows, masked, (((1,), (1,)), ((), ())), preferred_ele...  14 us
    unnamed x12, local copies, waits for them, and re-layouts  11.8 us
    mul x1, local copies, waits for them, and re-layouts, local(): partial_grad.reshape(blk_rows, 128, blk_cols, 128)  7.94 us
  transfers between devices with their start and end apart: 2, of which 2 were waited for; matrix products, arithmetic and copies ran while one was open for 22% of the time, Pallas kernels for 0%

commit v1 on v0

--- a/solution.py
+++ b/solution.py
@@ -1,9 +1,322 @@
+import functools
 import math
 
 import jax
 import jax.numpy as jnp
 from jax import lax
+from jax.experimental import pallas as pl
+from jax.experimental.pallas import tpu as pltpu
 from jax.sharding import PartitionSpec as P
+
+BLOCK = 128
+ORDER = (0, 1, 3, 2)
+
+
+def remote(src, dst, sends, recvs, at, device):
+    return pltpu.make_async_remote_copy(
+        src_ref=src,
+        dst_ref=dst,
+        send_sem=sends.at[at],
+        recv_sem=recvs.at[at],
+        device_id=device,
+        device_id_type=pl.DeviceIdType.MESH,
+    )
+
+
+def fused_kernel(
+    scale,
+    gate_hbm, up_hbm, weight_hbm, mask_ref, grad_hbm,
+    out_hbm, gate_grad_hbm, up_grad_hbm, weight_grad_hbm,
+    gate, up, weight, cot, hidden, hidden_t, partial,
+    first, second, third, send_second, send_third, final, gate_grad, up_grad, tile_out,
+    in_sem, out_sem, tile_sem,
+    z_send, z_recv, hop1_send, hop1_recv, hop2_send, hop2_recv, core_send, core_recv,
+    sum1_send, sum1_recv, sum2_send, sum2_recv, sum3_send, sum3_recv,
+):
+    d = lax.axis_index("dp")
+    t = lax.axis_index("tensor")
+    x = t % 2
+    y = (t // 2) % 2
+    z = t // 4
+    ff, width = weight.shape
+    tokens = gate.shape[0]
+    half = width // 2
+    halves = (pl.ds(0, half), pl.ds(half, half))
+    zs = [z] + [(z + k) % 4 for k in (1, 2, 3)]
+    x_peer = {"tensor": z * 4 + y * 2 + (1 - x)}
+    y_peer = {"tensor": z * 4 + (1 - y) * 2 + x}
+    core_peer = {"dp": 1 - d}
+    z_peer = [None] + [{"tensor": zs[k] * 4 + y * 2 + x} for k in (1, 2, 3)]
+
+    loads = [
+        pltpu.make_async_copy(gate_hbm, gate, in_sem.at[0]),
+        pltpu.make_async_copy(up_hbm, up, in_sem.at[1]),
+        pltpu.make_async_copy(weight_hbm.at[:, halves[0]], weight.at[:, halves[0]], in_sem.at[2]),
+        pltpu.make_async_copy(weight_hbm.at[:, halves[1]], weight.at[:, halves[1]], in_sem.at[3]),
+        pltpu.make_async_copy(grad_hbm, cot.at[d, z, y, x], in_sem.at[4]),
+    ]
+    for copy in loads:
+        copy.start()
+
+    barrier = pltpu.get_barrier_semaphore()
+    peers = [x_peer, y_peer, core_peer] + z_peer[1:]
+    for peer in peers:
+        pl.semaphore_signal(barrier, inc=1, device_id=peer, device_id_type=pl.DeviceIdType.MESH)
+    pl.semaphore_wait(barrier, len(peers))
+
+    along_z = {}
+    for k in (1, 3, 2):
+        along_z[k] = remote(grad_hbm, cot.at[d, z, y, x], z_send, z_recv, k - 1, z_peer[k])
+        along_z[k].start()
+    hop1, hop2, to_core = {}, {}, {}
+
+    def start_hop1(k):
+        at = zs[(4 - k) % 4]
+        for h, peer in enumerate((x_peer, y_peer)):
+            dst = cot.at[d, at, y, x, :, halves[h]]
+            src = grad_hbm.at[:, halves[h]] if k == 0 else dst
+            hop1[k, h] = remote(src, dst, hop1_send, hop1_recv, 2 * k + h, peer)
+            hop1[k, h].start()
+
+    def start_hop2(k):
+        at = zs[(4 - k) % 4]
+        refs = (cot.at[d, at, y, :, :, halves[0]], cot.at[d, at, :, x, :, halves[1]])
+        for h, peer in enumerate((y_peer, x_peer)):
+            hop1[k, h].wait_recv()
+        for h, peer in enumerate((y_peer, x_peer)):
+            hop2[k, h] = remote(refs[h], refs[h], hop2_send, hop2_recv, 2 * k + h, peer)
+            hop2[k, h].start()
+
+    def start_core(k):
+        at = zs[(4 - k) % 4]
+        for h in range(2):
+            hop2[k, h].wait_recv()
+        to_core[k] = remote(cot.at[d, at], cot.at[d, at], core_send, core_recv, k, core_peer)
+        to_core[k].start()
+
+    start_hop1(0)
+
+    loads[0].wait()
+    loads[1].wait()
+
+    def hidden_step(step, _):
+        cols = pl.ds(pl.multiple_of(step * 128, 128), 128)
+        g = gate[:, cols].astype(jnp.float32)
+        u = up[:, cols].astype(jnp.float32)
+        value = g * jax.nn.sigmoid(g) * u
+        hidden[:, cols] = value.astype(jnp.bfloat16)
+        hidden_t[d, cols, :] = value.T.astype(jnp.bfloat16)
+        return 0
+
+    lax.fori_loop(0, ff // 128, hidden_step, 0)
+    hidden_core = remote(hidden_t.at[d], hidden_t.at[d], core_send, core_recv, 4, core_peer)
+    hidden_core.start()
+
+    def forward(h):
+        wide = 512
+
+        def step(i, _):
+            cols = pl.ds(pl.multiple_of(h * half + i * wide, wide), wide)
+            for b in range(ff // BLOCK):
+                rows = pl.ds(b * BLOCK, BLOCK)
+                keep = jnp.broadcast_to(mask_ref[b : b + 1, cols], (BLOCK, wide))
+                weight[rows, cols] = weight[rows, cols] * keep.astype(jnp.bfloat16)
+            part = jnp.dot(hidden[...], weight[:, cols], preferred_element_type=jnp.float32)
+            partial[:, :, :, :, cols] = part.astype(jnp.bfloat16).reshape(
+                partial.shape[:4] + (wide,)
+            )
+            return 0
+
+        lax.fori_loop(0, half // wide, step, 0)
+
+    sum1, sum2, sum3 = {}, {}, {}
+
+    def start_sum1(h):
+        for k in (1, 3, 2, 0):
+            at = zs[k]
+            src = (partial.at[at, :, 1 - x, :, halves[0]], partial.at[at, 1 - y, :, :, halves[1]])[h]
+            sum1[k, h] = remote(
+                src, first.at[h, k], sum1_send, sum1_recv, 2 * k + h, (x_peer, y_peer)[h]
+            )
+            sum1[k, h].start()
+
+    loads[2].wait()
+    forward(0)
+    start_sum1(0)
+    for k in (1, 3):
+        along_z[k].wait_recv()
+        start_hop1(k)
+    loads[3].wait()
+    forward(1)
+    start_sum1(1)
+    along_z[2].wait_recv()
+    start_hop1(2)
+    loads[4].wait()
+    for k in ORDER:
+        start_hop2(k)
+
+    for k in (1, 3, 2, 0):
+        at = zs[k]
+        for h in range(2):
+            sum1[k, h].wait_recv()
+            other = (1 - y, 1 - x)[h]
+            mine = (partial[at, 1 - y, x, :, halves[0]], partial[at, y, 1 - x, :, halves[1]])[h]
+            total = mine.astype(jnp.float32) + first[h, k, other].astype(jnp.float32)
+            send_second[h, k] = total.astype(jnp.bfloat16)
+            sum2[k, h] = remote(
+                send_second.at[h, k], second.at[h, k], sum2_send, sum2_recv, 2 * k + h,
+                (y_peer, x_peer)[h],
+            )
+            sum2[k, h].start()
+
+    for k in ORDER:
+        start_core(k)
+
+    def own_total(k, h):
+        mine = partial[zs[k], y, x, :, halves[h]].astype(jnp.float32)
+        near = first[h, k, (y, x)[h]].astype(jnp.float32)
+        return mine + near + second[h, k].astype(jnp.float32)
+
+    for k in (1, 3, 2):
+        for h in range(2):
+            sum2[k, h].wait_recv()
+            send_third[h, k - 1] = own_total(k, h).astype(jnp.bfloat16)
+            sum3[k, h] = remote(
+                send_third.at[h, k - 1], third.at[h, k - 1], sum3_send, sum3_recv, 2 * k + h - 2,
+                z_peer[k],
+            )
+            sum3[k, h].start()
+
+    def grad_step(i, _):
+        wide = 256
+        rows = pl.ds(pl.multiple_of(i * wide, wide), wide)
+        rows_out = cot[d].reshape(tokens, width)
+        back = lax.dot_general(
+            rows_out, weight[rows, :], (((1,), (1,)), ((), ())), preferred_element_type=jnp.float32
+        )
+        g = gate[:, rows].astype(jnp.float32)
+        u = up[:, rows].astype(jnp.float32)
+        s = jax.nn.sigmoid(g)
+        gate_grad[:, rows] = (back * u * s * (1.0 + g * (1.0 - s))).astype(jnp.bfloat16)
+        up_grad[:, rows] = (back * (g * s)).astype(jnp.bfloat16)
+        return 0
+
+    lax.fori_loop(0, ff // 256, grad_step, 0)
+    stores = [
+        pltpu.make_async_copy(gate_grad, gate_grad_hbm, out_sem.at[0]),
+        pltpu.make_async_copy(up_grad, up_grad_hbm, out_sem.at[1]),
+    ]
+    for copy in stores:
+        copy.start()
+
+    hidden_core.wait_recv()
+    for k in ORDER:
+        to_core[k].wait_recv()
+
+    wide = 512
+
+    def tile_copy(slot, i):
+        cols = pl.ds(pl.multiple_of(i * wide, wide), wide)
+        return pltpu.make_async_copy(
+            tile_out.at[slot], weight_grad_hbm.at[:, cols], tile_sem.at[slot]
+        )
+
+    def weight_step(j, _):
+        for slot in range(2):
+            i = 2 * j + slot
+            cols = pl.ds(pl.multiple_of(i * wide, wide), wide)
+
+            @pl.when(j > 0)
+            def _():
+                tile_copy(slot, i - 2).wait()
+
+            total = jnp.zeros((ff, wide), jnp.float32)
+            for core in range(2):
+                total = total + jnp.dot(
+                    hidden_t[core],
+                    cot[core, :, :, :, :, cols].reshape(tokens, wide),
+                    preferred_element_type=jnp.float32,
+                )
+            for b in range(ff // BLOCK):
+                keep = mask_ref[b : b + 1, cols] * scale
+                tile_out[slot, pl.ds(b * BLOCK, BLOCK), :] = (
+                    total[b * BLOCK : (b + 1) * BLOCK] * keep
+                ).astype(jnp.bfloat16)
+            tile_copy(slot, i).start()
+        return 0
+
+    steps = width // wide
+    lax.fori_loop(0, steps // 2, weight_step, 0)
+
+    for h in range(2):
+        sum2[0, h].wait_recv()
+        total = own_total(0, h)
+        for k in (1, 2, 3):
+            sum3[k, h].wait_recv()
+            total = total + third[h, k - 1].astype(jnp.float32)
+        final[:, halves[h]] = total.astype(jnp.bfloat16)
+    stores.append(pltpu.make_async_copy(final, out_hbm, out_sem.at[2]))
+    stores[-1].start()
+
+    for copies in (along_z, hop1, hop2, to_core, sum1, sum2, sum3):
+        for copy in copies.values():
+            copy.wait_send()
+    hidden_core.wait_send()
+    for copy in stores:
+        copy.wait()
+    tile_copy(0, steps - 2).wait()
+    tile_copy(1, steps - 1).wait()
+
+
+def fused(gate_pre, up_pre, down_weight, block_mask, out_grad):
+    tokens, ff = gate_pre.shape
+    rows, width = out_grad.shape
+    half = width // 2
+    scale = 1.0 / math.sqrt(tokens * 2)
+    mask_rows = jnp.repeat(block_mask.astype(jnp.float32), BLOCK, axis=1)
+    hbm = pl.BlockSpec(memory_space=pl.ANY)
+    bf16 = jnp.bfloat16
+    dma = pltpu.SemaphoreType.DMA
+    counts = [3, 8, 8, 5, 8, 8, 6]
+    return pl.pallas_call(
+        functools.partial(fused_kernel, scale),
+        out_shape=(
+            jax.ShapeDtypeStruct((rows, width), bf16),
+            jax.ShapeDtypeStruct((tokens, ff), bf16),
+            jax.ShapeDtypeStruct((tokens, ff), bf16),
+            jax.ShapeDtypeStruct((ff, width), bf16),
+        ),
+        in_specs=[hbm, hbm, hbm, pl.BlockSpec(memory_space=pltpu.VMEM), hbm],
+        out_specs=(hbm,) * 4,
+        scratch_shapes=[
+            pltpu.VMEM((tokens, ff), bf16),
+            pltpu.VMEM((tokens, ff), bf16),
+            pltpu.VMEM((ff, width), bf16),
+            pltpu.VMEM((2, 4, 2, 2, rows, width), bf16),
+            pltpu.VMEM((tokens, ff), bf16),
+            pltpu.VMEM((2, ff, tokens), bf16),
+            pltpu.VMEM((4, 2, 2, rows, width), bf16),
+            pltpu.VMEM((2, 4, 2, rows, half), bf16),
+            pltpu.VMEM((2, 4, rows, half), bf16),
+            pltpu.VMEM((2, 3, rows, half), bf16),
+            pltpu.VMEM((2, 4, rows, half), bf16),
+            pltpu.VMEM((2, 3, rows, half), bf16),
+            pltpu.VMEM((rows, width), bf16),
+            pltpu.VMEM((tokens, ff), bf16),
+            pltpu.VMEM((tokens, ff), bf16),
+            pltpu.VMEM((2, ff, 512), bf16),
+            dma((5,)),
+            dma((3,)),
+            dma((2,)),
+        ]
+        + [dma((count,)) for count in counts for _ in range(2)],
+        compiler_params=pltpu.CompilerParams(
+            collective_id=0, has_side_effects=True, vmem_limit_bytes=60 * 2**20
+        ),
+        cost_estimate=pl.CostEstimate(
+            flops=8 * tokens * ff * width, bytes_accessed=40 * 2**20, transcendentals=2 * tokens * ff
+        ),
+    )(gate_pre, up_pre, down_weight, mask_rows, out_grad)
 
 
 def local(gate_pre, up_pre, down_weight, block_mask, out_grad):
@@ -50,8 +363,9 @@
 
 
 def solution(mesh):
+    grouped = mesh.shape["dp"] == 2 and mesh.shape["tensor"] == 16
     return jax.shard_map(
-        local,
+        fused if grouped else local,
         mesh=mesh,
         in_specs=(
             P("dp", "tensor"),

time: 279 us -> 115 us (0.41)
  waiting for transfers between devices: 148 us -> 0 us
  Pallas kernels: 0 us -> 98.7 us
  matrix products: 46.3 us -> 0 us
  blocking collectives: 46.2 us -> 0 us
  between operations: 14.1 us -> 0.64 us
  local copies, waits for them, and re-layouts: 20.9 us -> 14.9 us
    pallas_call x0 -> x1, Pallas kernels: none -> 98.7 us  [fused(): pl.pallas_call(functools.partial(fused_kernel, scale), out_shape=(jax.Sha...]
    reduce_scatter x1 -> x0, waiting for transfers between devices: 89.8 us -> none  [local(): lax.psum_scatter(jnp.dot(hidden, masked, preferred_element_type=jnp.float...]
    all_gather x1 -> x0, waiting for transfers between devices: 57.1 us -> none  [local(): cot_rows = lax.all_gather(out_grad, 'tensor', axis=0, tiled=True)]
    dot_general x3 -> x0, matrix products: 46.3 us -> none  [the longest x1 17.3 us: local(): lax.dot_general(hidden, cot_rows, (((0,), (0,)), ((), ())), preferred_ele...]
    psum x1 -> x0, blocking collectives: 46.2 us -> none  [local(): summed = lax.psum(blocked.reshape(ff_local, width), 'dp')]
    mul x2 -> x0, local copies, waits for them, and re-layouts: 9.09 us -> none  [the longest x1 7.94 us: local(): partial_grad.reshape(blk_rows, 128, blk_cols, 128)]
    unnamed x12 -> x4, local copies, waits for them, and re-layouts: 11.8 us -> 14.1 us
  transfers between devices with their start and end apart: 2 -> 0, of which waited for: 2 -> 0; matrix products, arithmetic and copies ran while one was open for 22% -> 0% of each run, Pallas kernels for 0% -> 0%
where the time goes in v1:
time: 115 us
  Pallas kernels  98.7 us (86%)
  local copies, waits for them, and re-layouts  14.9 us (13%)
    pallas_call x1, Pallas kernels, fused(): pl.pallas_call(functools.partial(fused_kernel, scale), out_shape=(jax.Sha...  98.7 us
    unnamed x4, local copies, waits for them, and re-layouts  14.1 us

profile of v1, /device:TPU:0, one launch (start us, length us, event | category | flops | bytes accessed | tf_op | source)
XLA Modules:
  0.0 115.0 jit_solution(6573017871564686722)
XLA Ops:
  0.6 0.7 convert_element_type.3
  1.3 0.1 copy.9
  1.4 0.8 broadcast_bitcast_fusion.mask_ref
  2.2 98.7 %shard_map.84 = (bf16[32,4096]{1,0:T(8,128)(2,1)}, bf16[512,1024]{1,0:T(8,128)(2,1)}, bf16[512,1024]{1,0:T(8,128)(2,1)}, bf16[1024,4096]{1,0:T(8,128)(2,1)}) custom-call(bf16[512,1024]{1,0:T(8,128)(2,1)} %gate_hbm.1, bf16[512,1024]{1,0:T(8,128)(2,1)} %up_hbm.1, bf16[1024,4096]{1,0:T(8,128)(2,1)} %weight_hbm.1, f32[8,4096]{1,0:T(8,128)} %broadcast_bitcast_fusion.mask_ref, ...), custom_call_target="tpu_custom_call" | custom-call | flops 17179869184 | bytes 41943040 | tf_op jit(solution)/shard_map/pallas_call | solution.py:281
  100.9 1.7 %copy.14 = bf16[32,4096]{1,0:T(8,128)(2,1)} copy(bf16[32,4096]{1,0:T(8,128)(2,1)} %get-tuple-element.8) | data formatting | bytes 524288
  102.6 2.3 %copy.15 = bf16[512,1024]{1,0:T(8,128)(2,1)} copy(bf16[512,1024]{1,0:T(8,128)(2,1)} %get-tuple-element.9) | data formatting | bytes 2097152
  104.8 2.3 %copy.16 = bf16[512,1024]{1,0:T(8,128)(2,1)} copy(bf16[512,1024]{1,0:T(8,128)(2,1)} %get-tuple-element.10) | data formatting | bytes 2097152
  107.1 7.9 %copy.17 = bf16[1024,4096]{1,0:T(8,128)(2,1)} copy(bf16[1024,4096]{1,0:T(8,128)(2,1)} %get-tuple-element.11) | data formatting | bytes 16777216

commit v2 on v1

--- a/solution.py
+++ b/solution.py
@@ -10,6 +10,7 @@
 
 BLOCK = 128
 ORDER = (0, 1, 3, 2)
+REST = 8
 
 
 def remote(src, dst, sends, recvs, at, device):
@@ -28,10 +29,12 @@
     gate_hbm, up_hbm, weight_hbm, mask_ref, grad_hbm,
     out_hbm, gate_grad_hbm, up_grad_hbm, weight_grad_hbm,
     gate, up, weight, cot, hidden, hidden_t, partial,
-    first, second, third, send_second, send_third, final, gate_grad, up_grad, tile_out,
+    first, second, third, send_second, send_third, final,
+    rest_third, rest_second, rest_first, send_rest_second, send_rest_first, gate_grad, up_grad, tile_out,
     in_sem, out_sem, tile_sem,
     z_send, z_recv, hop1_send, hop1_recv, hop2_send, hop2_recv, core_send, core_recv,
     sum1_send, sum1_recv, sum2_send, sum2_recv, sum3_send, sum3_recv,
+    rest_send, rest_recv, back_send, back_recv,
 ):
     d = lax.axis_index("dp")
     t = lax.axis_index("tensor")
@@ -40,8 +43,10 @@
     z = t // 4
     ff, width = weight.shape
     tokens = gate.shape[0]
-    half = width // 2
+    rest = width // REST
+    half = (width - rest) // 2
     halves = (pl.ds(0, half), pl.ds(half, half))
+    both, last = pl.ds(0, 2 * half), pl.ds(2 * half, rest)
     zs = [z] + [(z + k) % 4 for k in (1, 2, 3)]
     x_peer = {"tensor": z * 4 + y * 2 + (1 - x)}
     y_peer = {"tensor": z * 4 + (1 - y) * 2 + x}
@@ -51,8 +56,8 @@
     loads = [
         pltpu.make_async_copy(gate_hbm, gate, in_sem.at[0]),
         pltpu.make_async_copy(up_hbm, up, in_sem.at[1]),
-        pltpu.make_async_copy(weight_hbm.at[:, halves[0]], weight.at[:, halves[0]], in_sem.at[2]),
-        pltpu.make_async_copy(weight_hbm.at[:, halves[1]], weight.at[:, halves[1]], in_sem.at[3]),
+        pltpu.make_async_copy(weight_hbm.at[:, last], weight.at[:, last], in_sem.at[2]),
+        pltpu.make_async_copy(weight_hbm.at[:, both], weight.at[:, both], in_sem.at[3]),
         pltpu.make_async_copy(grad_hbm, cot.at[d, z, y, x], in_sem.at[4]),
     ]
     for copy in loads:
@@ -64,9 +69,16 @@
         pl.semaphore_signal(barrier, inc=1, device_id=peer, device_id_type=pl.DeviceIdType.MESH)
     pl.semaphore_wait(barrier, len(peers))
 
+    rest_x = remote(
+        grad_hbm.at[:, last], cot.at[d, z, y, x, :, last], rest_send, rest_recv, 0, x_peer
+    )
+    rest_x.start()
+    rest_z = {}
     along_z = {}
     for k in (1, 3, 2):
-        along_z[k] = remote(grad_hbm, cot.at[d, z, y, x], z_send, z_recv, k - 1, z_peer[k])
+        along_z[k] = remote(
+            grad_hbm.at[:, both], cot.at[d, z, y, x, :, both], z_send, z_recv, k - 1, z_peer[k]
+        )
         along_z[k].start()
     hop1, hop2, to_core = {}, {}, {}
 
@@ -91,6 +103,8 @@
         at = zs[(4 - k) % 4]
         for h in range(2):
             hop2[k, h].wait_recv()
+        if k:
+            rest_z[k].wait_recv()
         to_core[k] = remote(cot.at[d, at], cot.at[d, at], core_send, core_recv, k, core_peer)
         to_core[k].start()
 
@@ -112,22 +126,25 @@
     hidden_core = remote(hidden_t.at[d], hidden_t.at[d], core_send, core_recv, 4, core_peer)
     hidden_core.start()
 
-    def forward(h):
-        wide = 512
+    def forward(base, size):
+        wide = 256
 
         def step(i, _):
-            cols = pl.ds(pl.multiple_of(h * half + i * wide, wide), wide)
+            cols = pl.ds(pl.multiple_of(base + i * wide, BLOCK), wide)
             for b in range(ff // BLOCK):
                 rows = pl.ds(b * BLOCK, BLOCK)
-                keep = jnp.broadcast_to(mask_ref[b : b + 1, cols], (BLOCK, wide))
-                weight[rows, cols] = weight[rows, cols] * keep.astype(jnp.bfloat16)
+                for c in range(wide // BLOCK):
+                    at = pl.ds(pl.multiple_of(base + i * wide + c * BLOCK, BLOCK), BLOCK)
+                    keep = mask_ref[b, base // BLOCK + i * (wide // BLOCK) + c]
+                    keep = jnp.full((BLOCK, BLOCK), keep.astype(jnp.float32)).astype(jnp.bfloat16)
+                    weight[rows, at] = weight[rows, at] * keep
             part = jnp.dot(hidden[...], weight[:, cols], preferred_element_type=jnp.float32)
             partial[:, :, :, :, cols] = part.astype(jnp.bfloat16).reshape(
                 partial.shape[:4] + (wide,)
             )
             return 0
 
-        lax.fori_loop(0, half // wide, step, 0)
+        lax.fori_loop(0, size // wide, step, 0)
 
     sum1, sum2, sum3 = {}, {}, {}
 
@@ -140,22 +157,47 @@
             )
             sum1[k, h].start()
 
+    back_z = {}
+
+    def rest_sum(row, column):
+        total = partial[z, row, column, :, last].astype(jnp.float32)
+        for k in (1, 2, 3):
+            total = total + rest_third[k - 1, row, column].astype(jnp.float32)
+        return total
+
+    loads[4].wait()
+    rest_x.wait_recv()
+    rest_y = remote(
+        cot.at[d, z, y, :, :, last], cot.at[d, z, y, :, :, last], rest_send, rest_recv, 1, y_peer
+    )
+    rest_y.start()
     loads[2].wait()
-    forward(0)
+    forward(2 * half, rest)
+    for k in (1, 3, 2):
+        back_z[k] = remote(
+            partial.at[zs[k], :, :, :, last], rest_third.at[k - 1], back_send, back_recv, k - 1,
+            z_peer[k],
+        )
+        back_z[k].start()
+    loads[3].wait()
+    forward(0, half)
     start_sum1(0)
+    rest_y.wait_recv()
+    for k in (1, 3, 2):
+        rest_z[k] = remote(
+            cot.at[d, z, :, :, :, last], cot.at[d, z, :, :, :, last], rest_send, rest_recv, k + 1,
+            z_peer[k],
+        )
+        rest_z[k].start()
     for k in (1, 3):
         along_z[k].wait_recv()
         start_hop1(k)
-    loads[3].wait()
-    forward(1)
+    forward(half, half)
     start_sum1(1)
     along_z[2].wait_recv()
     start_hop1(2)
-    loads[4].wait()
-    for k in ORDER:
-        start_hop2(k)
-
-    for k in (1, 3, 2, 0):
+
+    def start_sum2(k):
         at = zs[k]
         for h in range(2):
             sum1[k, h].wait_recv()
@@ -169,15 +211,27 @@
             )
             sum2[k, h].start()
 
-    for k in ORDER:
-        start_core(k)
+    start_hop2(0)
+    start_hop2(1)
+    start_sum2(1)
+    start_hop2(3)
+    start_sum2(3)
+    start_hop2(2)
+    start_sum2(2)
+    start_sum2(0)
+    for k in (1, 2, 3):
+        back_z[k].wait_recv()
+    for column in range(2):
+        send_rest_second[column] = rest_sum(1 - y, column).astype(jnp.bfloat16)
+    back_y = remote(send_rest_second, rest_second, back_send, back_recv, 3, y_peer)
+    back_y.start()
 
     def own_total(k, h):
         mine = partial[zs[k], y, x, :, halves[h]].astype(jnp.float32)
         near = first[h, k, (y, x)[h]].astype(jnp.float32)
         return mine + near + second[h, k].astype(jnp.float32)
 
-    for k in (1, 3, 2):
+    def start_sum3(k):
         for h in range(2):
             sum2[k, h].wait_recv()
             send_third[h, k - 1] = own_total(k, h).astype(jnp.bfloat16)
@@ -186,6 +240,19 @@
                 z_peer[k],
             )
             sum3[k, h].start()
+
+    start_sum3(1)
+    start_core(0)
+    start_core(1)
+    start_sum3(3)
+    back_y.wait_recv()
+    total = rest_sum(y, 1 - x) + rest_second[1 - x].astype(jnp.float32)
+    send_rest_first[...] = total.astype(jnp.bfloat16)
+    back_x = remote(send_rest_first, rest_first, back_send, back_recv, 4, x_peer)
+    back_x.start()
+    start_core(3)
+    start_sum3(2)
+    start_core(2)
 
     def grad_step(i, _):
         wide = 256
@@ -238,10 +305,12 @@
                     preferred_element_type=jnp.float32,
                 )
             for b in range(ff // BLOCK):
-                keep = mask_ref[b : b + 1, cols] * scale
-                tile_out[slot, pl.ds(b * BLOCK, BLOCK), :] = (
-                    total[b * BLOCK : (b + 1) * BLOCK] * keep
-                ).astype(jnp.bfloat16)
+                for c in range(wide // BLOCK):
+                    keep = mask_ref[b, i * (wide // BLOCK) + c].astype(jnp.float32) * scale
+                    block = total[b * BLOCK : (b + 1) * BLOCK, c * BLOCK : (c + 1) * BLOCK]
+                    tile_out[slot, pl.ds(b * BLOCK, BLOCK), pl.ds(c * BLOCK, BLOCK)] = (
+                        block * keep
+                    ).astype(jnp.bfloat16)
             tile_copy(slot, i).start()
         return 0
 
@@ -255,13 +324,17 @@
             sum3[k, h].wait_recv()
             total = total + third[h, k - 1].astype(jnp.float32)
         final[:, halves[h]] = total.astype(jnp.bfloat16)
+    back_x.wait_recv()
+    total = rest_sum(y, x) + rest_second[x].astype(jnp.float32) + rest_first[...].astype(jnp.float32)
+    final[:, last] = total.astype(jnp.bfloat16)
     stores.append(pltpu.make_async_copy(final, out_hbm, out_sem.at[2]))
     stores[-1].start()
 
-    for copies in (along_z, hop1, hop2, to_core, sum1, sum2, sum3):
+    for copies in (along_z, hop1, hop2, to_core, sum1, sum2, sum3, rest_z, back_z):
         for copy in copies.values():
             copy.wait_send()
-    hidden_core.wait_send()
+    for copy in (hidden_core, rest_x, rest_y, back_y, back_x):
+        copy.wait_send()
     for copy in stores:
         copy.wait()
     tile_copy(0, steps - 2).wait()
@@ -271,14 +344,14 @@
 def fused(gate_pre, up_pre, down_weight, block_mask, out_grad):
     tokens, ff = gate_pre.shape
     rows, width = out_grad.shape
-    half = width // 2
+    rest = width // REST
+    half = (width - rest) // 2
     scale = 1.0 / math.sqrt(tokens * 2)
-    mask_rows = jnp.repeat(block_mask.astype(jnp.float32), BLOCK, axis=1)
     hbm = pl.BlockSpec(memory_space=pl.ANY)
     bf16 = jnp.bfloat16
     dma = pltpu.SemaphoreType.DMA
-    counts = [3, 8, 8, 5, 8, 8, 6]
-    return pl.pallas_call(
+    counts = [3, 8, 8, 5, 8, 8, 6, 5, 5]
+    results = pl.pallas_call(
         functools.partial(fused_kernel, scale),
         out_shape=(
             jax.ShapeDtypeStruct((rows, width), bf16),
@@ -286,7 +359,7 @@
             jax.ShapeDtypeStruct((tokens, ff), bf16),
             jax.ShapeDtypeStruct((ff, width), bf16),
         ),
-        in_specs=[hbm, hbm, hbm, pl.BlockSpec(memory_space=pltpu.VMEM), hbm],
+        in_specs=[hbm, hbm, hbm, pl.BlockSpec(memory_space=pltpu.SMEM), hbm],
         out_specs=(hbm,) * 4,
         scratch_shapes=[
             pltpu.VMEM((tokens, ff), bf16),
@@ -302,6 +375,11 @@
             pltpu.VMEM((2, 4, rows, half), bf16),
             pltpu.VMEM((2, 3, rows, half), bf16),
             pltpu.VMEM((rows, width), bf16),
+            pltpu.VMEM((3, 2, 2, rows, rest), bf16),
+            pltpu.VMEM((2, rows, rest), bf16),
+            pltpu.VMEM((rows, rest), bf16),
+            pltpu.VMEM((2, rows, rest), bf16),
+            pltpu.VMEM((rows, rest), bf16),
             pltpu.VMEM((tokens, ff), bf16),
             pltpu.VMEM((tokens, ff), bf16),
             pltpu.VMEM((2, ff, 512), bf16),
@@ -316,7 +394,47 @@
         cost_estimate=pl.CostEstimate(
             flops=8 * tokens * ff * width, bytes_accessed=40 * 2**20, transcendentals=2 * tokens * ff
         ),
-    )(gate_pre, up_pre, down_weight, mask_rows, out_grad)
+    )(gate_pre, up_pre, down_weight, block_mask, out_grad)
+    return hand_on(results)
+
+
+def pieces_of(array):
+    count = max(1, array.size // 2**19)
+    return [(piece * (array.shape[0] // count), array.shape[0] // count) for piece in range(count)]
+
+
+def hand_on_kernel(arrays, *refs):
+    srcs, dsts = refs[:arrays], refs[arrays : 2 * arrays]
+    held = refs[2 * arrays : 3 * arrays]
+    load_sem, store_sem = refs[3 * arrays :]
+    loads, stores = [], []
+    for src, dst, hold in zip(srcs, dsts, held):
+        for first_row, rows in pieces_of(src):
+            at = pl.ds(first_row, rows)
+            n = len(loads)
+            loads.append(pltpu.make_async_copy(src.at[at], hold.at[at], load_sem.at[n]))
+            stores.append(pltpu.make_async_copy(hold.at[at], dst.at[at], store_sem.at[n]))
+    for load in loads:
+        load.start()
+    for load, store in zip(loads, stores):
+        load.wait()
+        store.start()
+    for store in stores:
+        store.wait()
+
+
+def hand_on(arrays):
+    hbm = pl.BlockSpec(memory_space=pl.ANY)
+    count = sum(len(pieces_of(a)) for a in arrays)
+    return pl.pallas_call(
+        functools.partial(hand_on_kernel, len(arrays)),
+        out_shape=tuple(jax.ShapeDtypeStruct(a.shape, a.dtype) for a in arrays),
+        in_specs=[hbm] * len(arrays),
+        out_specs=(hbm,) * len(arrays),
+        scratch_shapes=[pltpu.VMEM(a.shape, a.dtype) for a in arrays]
+        + [pltpu.SemaphoreType.DMA((count,))] * 2,
+        compiler_params=pltpu.CompilerParams(vmem_limit_bytes=60 * 2**20),
+    )(*arrays)
 
 
 def local(gate_pre, up_pre, down_weight, block_mask, out_grad):

time: 115 us -> 103 us (0.90)
  local copies, waits for them, and re-layouts: 14.9 us -> 0 us
  Pallas kernels: 98.7 us -> 102 us
    unnamed x4 -> x0, local copies, waits for them, and re-layouts: 14.1 us -> none
    pallas_call x0 -> x1, Pallas kernels: none -> 8.37 us  [hand_on(): pl.pallas_call(functools.partial(hand_on_kernel, len(arrays)), out_shape=...]
    pallas_call x1, Pallas kernels: 98.7 us -> 94 us  [fused(): pl.pallas_call(functools.partial(fused_kernel, scale), out_shape=(jax.Sha...]
where the time goes in v2:
time: 103 us
  Pallas kernels  102 us (99%)
    pallas_call x1, Pallas kernels, fused(): pl.pallas_call(functools.partial(fused_kernel, scale), out_shape=(jax.Sha...  94 us
    pallas_call x1, Pallas kernels, hand_on(): pl.pallas_call(functools.partial(hand_on_kernel, len(arrays)), out_shape=...  8.37 us

profile of v2, /device:TPU:0, one launch (start us, length us, event | category | flops | bytes accessed | tf_op | source)
XLA Modules:
  0.0 103.0 jit_solution(6433902868926645522)
XLA Ops:
  0.6 94.0 %shard_map.84 = (bf16[32,4096]{1,0:T(8,128)(2,1)}, bf16[512,1024]{1,0:T(8,128)(2,1)}, bf16[512,1024]{1,0:T(8,128)(2,1)}, bf16[1024,4096]{1,0:T(8,128)(2,1)}) custom-call(bf16[512,1024]{1,0:T(8,128)(2,1)} %gate_hbm.1, bf16[512,1024]{1,0:T(8,128)(2,1)} %up_hbm.1, bf16[1024,4096]{1,0:T(8,128)(2,1)} %weight_hbm.1, s32[8,32]{1,0:T(8,128)} %mask_ref.1, ...), custom_call_target="tpu_custom_call" | custom-call | flops 17179869184 | bytes 41943040 | tf_op jit(solution)/shard_map/pallas_call | solution.py:354
  94.6 8.4 %shard_map.85 = (bf16[32,4096]{1,0:T(8,128)(2,1)}, bf16[512,1024]{1,0:T(8,128)(2,1)}, bf16[512,1024]{1,0:T(8,128)(2,1)}, bf16[1024,4096]{1,0:T(8,128)(2,1)}) custom-call(bf16[32,4096]{1,0:T(8,128)(2,1)} %get-tuple-element.8.refs_0_, bf16[512,1024]{1,0:T(8,128)(2,1)} %get-tuple-element.9.refs_1_, bf16[512,1024]{1,0:T(8,128)(2,1)} %get-tuple-element.10.refs_2_, ...), custom_call_target="tpu_custom_call" | custom-call | tf_op jit(solution)/shard_map/pallas_call | solution.py:429
